TPU v7x, 32 devices: a whole 2x2x4 slice. The times are simulated.
32 devices in a mesh: parts: 2 (over x), req: 2 (over core), tp: 8 (over z, y).
Axes of the slice: x: 2, y: 2, z: 4, core: 2. Of those that a mesh axis runs over, the one named last changes fastest.
Arguments:
- input_hidden_rows: bfloat16 [64, 8192], P(('parts', 'req')), parts along dimension 0, may hold values from -6 to 6
- input_norm_scale: bfloat16 [8192], replicated, may hold values from 0.099609375 to 1.8984375
- query_weight: bfloat16 [8192, 4096], P(None, 'tp'), may hold values from -0.0625 to 0.0625
- key_value_weight: bfloat16 [8192, 1024], P(None, 'tp'), may hold values from -0.0625 to 0.0625
- output_weight: bfloat16 [4096, 8192], P('tp'), may hold values from -0.125 to 0.125
- cache: bfloat16 [64, 512, 1024], P(('parts', 'req', 'tp')), parts along dimension 0, may hold values from -2000 to 2000
- lengths: int32 [64], P(('parts', 'req', 'tp')), parts along dimension 0, may hold values from 2 to 512, as said below
- adapter_per_block: int32 [4], P(('parts', 'req')), parts along dimension 0, may hold values from 0 to 127
- adapter_storage_slot: int32 [128], replicated, may hold values from 0 to 127, each once
- adapter_down_projection: bfloat16 [128, 16, 4096], P('req', None, 'tp'), may hold values from -0.09375 to 0.09375
- adapter_up_projection: bfloat16 [128, 16, 8192], P('req', None, 'tp'), may hold values from -3 to 3
Outputs:
- hidden_out: bfloat16 [64, 8192], P(('parts', 'req')), parts along dimension 0
- new_pairs: bfloat16 [2, 64, 1024], P(None, ('parts', 'req', 'tp')), parts along dimension 1
There are 2 independent parts, one for each index of `parts`. A program takes and returns all parts, laid end to end along the dimension named above; an argument that names none is the same for every part. Nothing has to cross between parts.
Inputs may be any that keep to these rules, and one draw needn't show every extreme that they name: `lengths`: each row has at least two valid positions and some row of every draw has 512.
All inputs are finite; a program needn't handle non-finite values.
Results may differ from a plain program's by a relative error of at most 0.025.
The roundings to bfloat16 on the way count: a program that leaves them out, or rounds other values in their place, can miss the bound.
Values may be sent and summed in bfloat16 or wider, within the bound.
No kernel may reach another device: no remote copies, remote signals or barrier semaphores. Data moves between devices by JAX's collectives and lax.ppermute only.
A program may use at most 128 MiB of HBM per device.

v0:
```python
import math

import jax
import jax.numpy as jnp
from jax import lax
from jax.experimental import pallas as pl
from jax.experimental.pallas import tpu as pltpu
from jax.sharding import PartitionSpec as P

MODEL_WIDTH = 8192
HEAD_SIZE = 128
QUERY_HEAD_COUNT = 32
KV_HEADS = 4
BLOCK = 16
STEPS = 2

rope_base = 500000.0
norm_epsilon = 1e-05
term_type = jnp.bfloat16
f32 = jnp.float32
bf16 = jnp.bfloat16
MIB = 1 << 20


def whole(kind=pltpu.VMEM):
    return pl.BlockSpec(memory_space=kind)


def call(body, outs, ins, flops, data_bytes, limit=16):
    return pl.pallas_call(
        body,
        out_shape=outs,
        in_specs=ins,
        out_specs=jax.tree.map(lambda _: whole(), outs),
        compiler_params=pltpu.CompilerParams(vmem_limit_bytes=limit * MIB),
        cost_estimate=pl.CostEstimate(flops=flops, bytes_accessed=data_bytes, transcendentals=0),
    )


def far(array):
    return pltpu.with_memory_space_constraint(array, pltpu.HBM)


def rows_of(ref, start, width):
    pieces = [ref[j, :, pl.ds(start, width)].astype(f32) for j in range(ref.shape[0])]
    return jnp.concatenate(pieces, axis=0).astype(bf16)


def pieces_of(depth, count):
    return [(i * depth // count, (i + 1) * depth // count) for i in range(count)]


def project(weights, chunk_of, rows, pieces, ready=None):
    sums = [jnp.zeros((rows, w.shape[1]), f32) for w in weights]
    for i, (start, stop) in enumerate(pieces):
        if ready is not None:
            ready(i)
        part = chunk_of(start, stop - start)
        sums = [
            total + jnp.dot(part, w[start:stop, :], preferred_element_type=f32)
            for total, w in zip(sums, weights)
        ]
    return sums


def store_shares(out, query, pair):
    shares, own, _ = out.shape
    width = query.shape[1]
    for j in range(shares):
        lines = slice(j * own, (j + 1) * own)
        out[j, :, :width] = query[lines].astype(bf16)
        out[j, :, width:] = pair[lines].astype(bf16)


def cost(flops, data_bytes):
    return pl.CostEstimate(flops=flops, bytes_accessed=data_bytes, transcendentals=0)


def first_projection(source, scale, weights, own):
    rows, width = source.shape
    shares = rows // own
    message = sum(w.shape[1] for w in weights)
    pieces = pieces_of(width, 4)
    ahead = 2

    def body(mine, source_ref, s, wq, wp, out, held, *scratch):
        kept_q, kept_p, sems, x, gains, wide, normed, pre = scratch
        loads = [
            pltpu.make_async_copy(source_ref, x, pre.at[0]),
            pltpu.make_async_copy(s, gains, pre.at[1]),
        ]
        for load in loads:
            load.start()
        copies = [
            [
                pltpu.make_async_copy(w.at[start:stop, :], k.at[start:stop, :], sems.at[n, i])
                for n, (w, k) in enumerate(((wq, kept_q), (wp, kept_p)))
            ]
            for i, (start, stop) in enumerate(pieces)
        ]
        for pair in copies[:ahead]:
            for copy in pair:
                copy.start()

        def ready(i):
            for copy in copies[i]:
                copy.wait()
            for copy in copies[i + ahead] if i + ahead < len(copies) else []:
                copy.start()

        for load in loads:
            load.wait()
        wide[...] = x[...].astype(f32)
        lines = wide[:own, :]
        for j in range(1, shares):
            lines = jnp.where(mine[0] == j, wide[j * own : (j + 1) * own, :], lines)
        held[...] = lines.astype(bf16)
        value = wide[...]
        ratio = lax.rsqrt(jnp.mean(value * value, axis=-1, keepdims=True) + norm_epsilon)
        gain = gains[...].astype(f32)
        for c in range(width // HEAD_SIZE):
            columns = slice(c * HEAD_SIZE, (c + 1) * HEAD_SIZE)
            normed[:, columns] = (wide[:, columns] * ratio * gain[c : c + 1, :]).astype(bf16)
        sums = project(
            (kept_q, kept_p), lambda at, n: normed[:, at : at + n], rows, pieces, ready
        )
        store_shares(out, *sums)

    return pl.pallas_call(
        body,
        out_shape=(
            jax.ShapeDtypeStruct((shares, own, message), bf16),
            jax.ShapeDtypeStruct((own, width), bf16),
        ),
        in_specs=[whole(pltpu.SMEM)] + [whole(pltpu.HBM)] * 4,
        out_specs=(whole(), whole()),
        scratch_shapes=[pltpu.VMEM(w.shape, bf16) for w in weights]
        + [
            pltpu.SemaphoreType.DMA((2, len(pieces))),
            pltpu.VMEM(source.shape, bf16),
            pltpu.VMEM(scale.shape, bf16),
            pltpu.VMEM(source.shape, f32),
            pltpu.VMEM(source.shape, bf16),
            pltpu.SemaphoreType.DMA((2,)),
        ],
        compiler_params=pltpu.CompilerParams(vmem_limit_bytes=24 * MIB),
        cost_estimate=cost(2 * rows * width * message, 2 * width * message),
    )(own_index("tp"), far(source), far(scale), *map(far, weights))


def next_projection(normed, weights):
    shares, own, width = normed.shape
    message = sum(w.shape[1] for w in weights)

    def body(x, wq, wp, out):
        pieces = pieces_of(width, 8)
        store_shares(out, *project((wq, wp), lambda at, n: rows_of(x, at, n), shares * own, pieces))

    return call(
        body,
        jax.ShapeDtypeStruct((shares, own, message), bf16),
        [whole()] * 3,
        2 * shares * own * width * message,
        2 * width * message,
    )(normed, *weights)


def own_index(axis):
    return lax.axis_index(axis).astype(jnp.int32).reshape(1)


def fetch(block, per_block, slots, side, here, other, target, sem):
    stored_here = here.shape[0]
    slot = slots[per_block[block]]
    at = lax.rem(slot, jnp.int32(stored_here))
    mine = lax.div(slot, jnp.int32(stored_here)) == side[0]

    @pl.when(mine)
    def _():
        pltpu.make_async_copy(here.at[at], target.at[block], sem.at[block]).start()

    @pl.when(jnp.logical_not(mine))
    def _():
        pltpu.make_async_copy(other.at[at], target.at[block], sem.at[block]).start()

    return pltpu.make_async_copy(here.at[0], target.at[block], sem.at[block])


def add_down(message, adapters, here, other, lengths, blocks):
    shares, own, width = message.shape
    _, rank, columns = here.shape
    lead = rank // own * columns

    def body(per_block, slots, side, lens, m, here_ref, other_ref, out, turns, piece, sem):
        waits = [
            fetch(b, per_block, slots, side, here_ref, other_ref, piece, sem)
            for b in range(blocks)
        ]
        for j in range(shares):
            out[j, :, lead:] = m[j]
        half_head = HEAD_SIZE // 2
        lane = lax.broadcasted_iota(jnp.int32, (STEPS * own, HEAD_SIZE), 1)
        line = lax.broadcasted_iota(jnp.int32, (STEPS * own, HEAD_SIZE), 0)
        position = jnp.zeros_like(line)
        for n in range(STEPS * own):
            position = jnp.where(line == n, lens[n % own] + n // own, position)
        entry = jnp.where(lane < half_head, lane, lane - half_head).astype(f32)
        angle = position.astype(f32) * jnp.exp(entry * f32(-2.0 / HEAD_SIZE * math.log(rope_base)))
        sine = jnp.sin(angle)
        turns[0] = jnp.cos(angle)
        turns[1] = jnp.where(lane < half_head, -sine, sine)
        for wait in waits:
            wait.wait()
        for b in range(blocks):
            lines = [
                piece[b, m * own : (m + 1) * own, :].astype(f32) for m in range(rank // own)
            ]
            packed = jnp.concatenate(lines, axis=1).astype(bf16)
            for j in range(b * BLOCK // own, (b + 1) * BLOCK // own):
                out[j, :, :lead] = packed

    smem = whole(pltpu.SMEM)
    return pl.pallas_call(
        body,
        out_shape=(
            jax.ShapeDtypeStruct((shares, own, lead + width), bf16),
            jax.ShapeDtypeStruct((2, STEPS * own, HEAD_SIZE), f32),
        ),
        in_specs=[smem] * 4 + [whole(), whole(pl.ANY), whole(pl.ANY)],
        out_specs=(whole(), whole()),
        scratch_shapes=[
            pltpu.VMEM((blocks, rank, columns), bf16),
            pltpu.SemaphoreType.DMA((blocks,)),
        ],
        compiler_params=pltpu.CompilerParams(vmem_limit_bytes=16 * MIB),
    )(*adapters, lengths, message, here, other)


def attend(arrived, pairs, older, turns, lengths, cache, adapters, stores, step, lead, rank):
    shares, own, message = arrived.shape
    context, width = cache.shape[1:]
    half = width // 2
    query_width = QUERY_HEAD_COUNT * HEAD_SIZE // shares
    per_share = query_width // HEAD_SIZE
    groups = QUERY_HEAD_COUNT // KV_HEADS
    lines = groups * own
    pair_inside = pairs is None
    first, last = step == 0, step == STEPS - 1
    shrink = 1.0 / math.sqrt(HEAD_SIZE)

    def body(*refs):
        refs = list(refs)
        lens, x = refs.pop(0), refs.pop(0)
        pair_ref = None if pair_inside else refs.pop(0)
        old = None if first else refs.pop(0)
        turn_ref, kv = refs.pop(0), refs.pop(0)
        if first:
            per_block, slots, side, here, other, out, new, down_ref, ups, sem = refs
            waits = [
                fetch(b, per_block, slots, side, here, other, ups, sem)
                for b in range(ups.shape[0])
            ]
            for j in range(shares):
                pieces = [
                    x[j, :, m * query_width : (m + 1) * query_width].astype(f32)
                    for m in range(rank // own)
                ]
                down_ref[j] = jnp.concatenate(pieces, axis=0).astype(bf16)
        else:
            down_ref, out, new = refs
        cosine = turn_ref[0, step * own : (step + 1) * own, :]
        sine = turn_ref[1, step * own : (step + 1) * own, :]
        row_of = lax.rem(lax.broadcasted_iota(jnp.int32, (lines, 1), 0), own)

        def by_row(values):
            result = values[0]
            for r in range(1, own):
                result = jnp.where(row_of == r, values[r], result)
            return result

        def spread(rows):
            return by_row([rows[r : r + 1, :] for r in range(own)])

        def turn(v, c, s):
            return v * c + pltpu.roll(v, HEAD_SIZE // 2, 1) * s

        def pair_head(c):
            if pair_inside:
                return x[c, :, lead + query_width :].astype(f32)
            return pair_ref[:, c * HEAD_SIZE : (c + 1) * HEAD_SIZE].astype(f32)

        keys = [turn(pair_head(g), cosine, sine).astype(bf16) for g in range(KV_HEADS)]
        values = [pair_head(KV_HEADS + g).astype(bf16) for g in range(KV_HEADS)]
        fresh = jnp.concatenate(keys + values, axis=1)
        if last:
            new[0] = old[...]
            new[1] = fresh
        else:
            new[...] = fresh
        wide_cosine, wide_sine = spread(cosine), spread(sine)
        valid = lax.broadcasted_iota(jnp.int32, (lines, context), 1) < by_row(
            [jnp.full((lines, 1), lens[r], jnp.int32) for r in range(own)]
        )
        scores = []
        extras = []
        new_values = []
        for g in range(KV_HEADS):
            column = slice(g * HEAD_SIZE, (g + 1) * HEAD_SIZE)
            value_column = slice(half + g * HEAD_SIZE, half + (g + 1) * HEAD_SIZE)
            pieces = []
            for h in range(g * groups, (g + 1) * groups):
                at = lead + (h % per_share) * HEAD_SIZE
                pieces.append(x[h // per_share, :, at : at + HEAD_SIZE].astype(f32))
            query = turn(jnp.concatenate(pieces, axis=0), wide_cosine, wide_sine).astype(bf16)
            score = by_row(
                [
                    lax.dot_general(
                        query, kv[r, :, column], (((1,), (1,)), ((), ())), preferred_element_type=f32
                    )
                    for r in range(own)
                ]
            )
            scores.append(jnp.where(valid, score * shrink, f32(-1e30)))
            added = [(keys[g], values[g])]
            if not first:
                added.append((old[:, column], old[:, value_column]))
            wide_query = query.astype(f32)
            extras.append(
                [
                    jnp.sum(wide_query * spread(k.astype(f32)), axis=1, keepdims=True) * shrink
                    for k, _ in added
                ]
            )
            new_values.append([spread(v.astype(f32)) for _, v in added])
        results = []
        for g in range(KV_HEADS):
            value_column = slice(half + g * HEAD_SIZE, half + (g + 1) * HEAD_SIZE)
            peak = jnp.max(scores[g], axis=1, keepdims=True)
            for e in extras[g]:
                peak = jnp.maximum(peak, e)
            weight = jnp.exp(scores[g] - peak)
            more = [jnp.exp(e - peak) for e in extras[g]]
            total = jnp.sum(weight, axis=1, keepdims=True)
            for e in more:
                total = total + e
            probs = (weight / total).astype(bf16)
            result = by_row(
                [
                    jnp.dot(probs, kv[r, :, value_column], preferred_element_type=f32)
                    for r in range(own)
                ]
            )
            for e, v in zip(more, new_values[g]):
                result = result + (e / total).astype(bf16).astype(f32) * v
            results.append(result)
        low = jnp.zeros((own, rank), f32)
        for j in range(shares):
            cells = []
            for h in range(j * per_share, (j + 1) * per_share):
                at = h % groups * own
                cells.append(results[h // groups][at : at + own, :])
            share = jnp.concatenate(cells, axis=1).astype(bf16)
            out[j, :, :query_width] = share
            low = low + lax.dot_general(
                share, down_ref[j], (((1,), (1,)), ((), ())), preferred_element_type=f32
            )
        padded = jnp.concatenate([low, jnp.zeros((own, HEAD_SIZE - rank), f32)], axis=1).astype(bf16)
        for j in range(shares):
            out[j, :, query_width:] = padded
        if first:
            for wait in waits:
                wait.wait()

    smem = whole(pltpu.SMEM)
    operands = [lengths, arrived]
    specs = [smem, whole()]
    for extra in ([] if pair_inside else [pairs]) + ([] if first else [older]) + [turns, cache]:
        operands.append(extra)
        specs.append(whole())
    outs = [
        jax.ShapeDtypeStruct((shares, own, query_width + HEAD_SIZE), bf16),
        jax.ShapeDtypeStruct((STEPS, own, width) if last else (own, width), bf16),
    ]
    scratch = []
    if first:
        operands += [*adapters, far(stores[0]), stores[1]]
        specs += [smem] * 3 + [whole(pltpu.HBM), whole(pl.ANY)]
        blocks = adapters[0].shape[0]
        outs.append(jax.ShapeDtypeStruct((shares, rank, query_width), bf16))
        outs.append(jax.ShapeDtypeStruct((blocks,) + stores[0].shape[1:], bf16))
        scratch.append(pltpu.SemaphoreType.DMA((blocks,)))
    else:
        operands.append(stores)
        specs.append(whole())
    return pl.pallas_call(
        body,
        out_shape=tuple(outs),
        in_specs=specs,
        out_specs=(whole(),) * len(outs),
        scratch_shapes=scratch,
        compiler_params=pltpu.CompilerParams(vmem_limit_bytes=16 * MIB),
        cost_estimate=cost(
            8 * own * QUERY_HEAD_COUNT * HEAD_SIZE * context, 2 * own * context * width
        ),
    )(*operands)


def output_terms(arrived, output_weight, up):
    shares, own, _ = arrived.shape
    query_width, width = output_weight.shape
    blocks, rank, share_width = up.shape
    rows = shares * own
    step = 1024

    def body(mine, x, wo, up_ref, out, added):
        heads = rows_of(x, 0, query_width)
        low = rows_of(x, query_width, HEAD_SIZE)[:, :rank]
        added[...] = jnp.zeros_like(added)
        start = pl.multiple_of(mine[0] * share_width, share_width)
        for b in range(blocks):
            lines = slice(b * BLOCK, (b + 1) * BLOCK)
            added[lines, pl.ds(start, share_width)] = jnp.dot(
                low[lines], up_ref[b], preferred_element_type=f32
            )
        for i in range(width // step):
            columns = slice(i * step, (i + 1) * step)
            total = added[:, columns] + jnp.dot(
                heads, wo[:, columns], preferred_element_type=f32
            )
            for j in range(shares):
                out[j, :, columns] = total[j * own : (j + 1) * own, :].astype(out.dtype)

    return pl.pallas_call(
        body,
        out_shape=jax.ShapeDtypeStruct((shares, own, width), term_type),
        in_specs=[whole(pltpu.SMEM)] + [whole()] * 3,
        out_specs=whole(),
        scratch_shapes=[pltpu.VMEM((rows, width), f32)],
        compiler_params=pltpu.CompilerParams(vmem_limit_bytes=16 * MIB),
        cost_estimate=cost(2 * rows * width * query_width, 2 * width * query_width),
    )(own_index("tp"), arrived, output_weight, up)


def close_step(terms, hidden, scale):
    shares, own, width = terms.shape
    normed = scale is not None

    def body(t, h, *refs):
        total = h[...].astype(f32)
        for j in range(shares):
            total = total + t[j].astype(f32)
        rounded = total.astype(bf16)
        spread = rounded
        if normed:
            s, out, kept = refs
            kept[...] = rounded
            wide = rounded.astype(f32)
            mean = jnp.mean(wide * wide, axis=-1, keepdims=True)
            wide = wide * lax.rsqrt(mean + norm_epsilon)
            gain = s[...].astype(f32)
            spread = jnp.concatenate(
                [
                    wide[:, c * HEAD_SIZE : (c + 1) * HEAD_SIZE] * gain[c : c + 1, :]
                    for c in range(width // HEAD_SIZE)
                ],
                axis=1,
            ).astype(bf16)
        else:
            (out,) = refs
        for j in range(shares):
            out[j] = spread

    outs = [jax.ShapeDtypeStruct((shares, own, width), bf16)]
    operands = [terms, hidden]
    if normed:
        outs.append(jax.ShapeDtypeStruct((own, width), bf16))
        operands.append(scale)
    return call(
        body, tuple(outs), [whole()] * len(operands), 8 * own * width, 6 * shares * own * width
    )(*operands)


def exchange(chunks):
    return lax.all_to_all(chunks, "tp", split_axis=0, concat_axis=0, tiled=True)


def local(
    input_hidden_rows,
    input_norm_scale,
    query_weight,
    key_value_weight,
    output_weight,
    cache,
    lengths,
    adapter_per_block,
    adapter_storage_slot,
    adapter_down_projection,
    adapter_up_projection,
):
    rows_req = input_hidden_rows.shape[0]
    own = cache.shape[0]
    blocks = rows_req // BLOCK
    width = input_hidden_rows.shape[1]
    query_width = query_weight.shape[1]
    rank = adapter_down_projection.shape[1]
    scale = input_norm_scale.reshape(width // HEAD_SIZE, HEAD_SIZE)
    adapters = (
        adapter_per_block,
        adapter_storage_slot,
        own_index("req"),
    )
    cores = [(0, 1), (1, 0)]
    other_down = lax.ppermute(adapter_down_projection, "req", cores)
    other_up = lax.ppermute(adapter_up_projection, "req", cores)
    lead = rank // own * query_width
    weights = (query_weight, key_value_weight)
    message, hidden = first_projection(input_hidden_rows, scale, weights, own)
    message, turns = add_down(
        message, adapters, adapter_down_projection, other_down, lengths, blocks
    )
    down = fresh = None
    for step in range(STEPS):
        arrived = exchange(message)
        start = 0 if step else lead
        pairs = None
        if key_value_weight.shape[1] != HEAD_SIZE:
            pairs = arrived[:, :, start + query_width :].transpose(1, 0, 2).reshape(own, -1)
        stores = down if step else (adapter_up_projection, other_up)
        attended, fresh, *kept = attend(
            arrived, pairs, fresh, turns, lengths, cache, adapters, stores, step, start, rank
        )
        if not step:
            down, up = kept
        terms = exchange(output_terms(exchange(attended), output_weight, up))
        if step < STEPS - 1:
            spread, hidden = close_step(terms, hidden, scale)
            message = next_projection(exchange(spread), weights)
        else:
            (spread,) = close_step(terms, hidden, None)
    return (exchange(spread).reshape(rows_req, width), fresh)


def solution(mesh):
    in_specs = (
        P(("parts", "req"), None),
        P(),
        P(None, "tp"),
        P(None, "tp"),
        P("tp", None),
        P(("parts", "req", "tp"), None, None),
        P(("parts", "req", "tp")),
        P(("parts", "req")),
        P(),
        P("req", None, "tp"),
        P("req", None, "tp"),
    )
    out_specs = (P(("parts", "req"), None), P(None, ("parts", "req", "tp"), None))
    return jax.shard_map(local, mesh=mesh, in_specs=in_specs, out_specs=out_specs, check_vma=False)
```

profile of v0, /device:TPU:0, one launch (start us, length us, event | category | flops | bytes accessed | tf_op | source)
XLA Modules:
  0.0 102.8 jit_solution(5147312849517334428)
XLA Ops:
  0.6 0.5 collective-permute-start.1
  1.1 0.1 collective-permute-start
  1.9 0.0 copy-start.3
  1.9 0.0 copy-start.5
  1.9 0.0 copy-start.6
  1.9 0.0 copy-start.1
  1.9 5.8 %shard_map.122 = (bf16[8,2,640]{2,1,0:T(2,128)(2,1)S(1)}, bf16[2,8192]{1,0:T(2,128)(2,1)S(1)}) custom-call(s32[1]{0:T(128)} %bitcast.mine, bf16[16,8192]{1,0:T(8,128)(2,1)} %source_ref.1, bf16[64,128]{1,0:T(8,128)(2,1)} %bitcast.5, bf16[8192,512]{1,0:T(8,128)(2,1)} %wq.3, bf16[8192,128]{1,0:T(8,128)(2,1)} %wp.3), custom_call_target="tpu_custom_call" | custom-call | flops 167772160 | bytes 10485760 | tf_op jit(solution)/shard_map/pallas_call | solution.py:129
  7.7 0.0 collective-permute-done.other_ref
  7.7 0.0 copy-done.3
  7.7 0.0 copy-done.5
  7.7 0.0 copy-done.6
  7.8 0.0 copy-start
  7.8 0.7 shard_map.123
  8.5 14.8 %all_to_all.40.refs_1_ = bf16[8,2,4736]{2,1,0:T(2,128)(2,1)S(1)} all-to-all(bf16[8,2,4736]{2,1,0:T(2,128)(2,1)S(1)} %get-tuple-element.15), channel_id=1, replica_groups=mesh['parts'=2,'req'=2,'tp'=8] {'tp'}, dimensions={0} | all-to-all | bytes 303104 | tf_op jit(solution)/shard_map/all_to_all | solution.py:484
  23.3 0.0 collective-permute-done.1.refs_8_
  23.3 0.0 copy-done.1
  23.3 0.0 copy-start.4
  23.3 0.0 slice-start
  23.3 1.6 %shard_map.124 = (bf16[8,2,640]{2,1,0:T(2,128)(2,1)S(1)}, bf16[2,1024]{1,0:T(2,128)(2,1)S(1)}, bf16[8,16,512]{2,1,0:T(8,128)(2,1)S(1)}, bf16[1,16,1024]{2,1,0:T(8,128)(2,1)S(1)}) custom-call(s32[2]{0:T(128)S(1)} %copy-done.5, bf16[8,2,4736]{2,1,0:T(2,128)(2,1)S(1)} %all_to_all.40.refs_1_, f32[2,4,128]{2,1,0:T(4,128)S(1)} %get-tuple-element.16.refs_2_.refs_3_, ...), custom_call_target="tpu_custom_call" | custom-call | flops 33554432 | bytes 2097152 | tf_op jit(solution)/shard_map/pallas_call | solution.py:395
  24.9 9.3 %all_to_all.41.x = bf16[8,2,640]{2,1,0:T(2,128)(2,1)S(1)} all-to-all(bf16[8,2,640]{2,1,0:T(2,128)(2,1)S(1)} %get-tuple-element.17), channel_id=1, replica_groups=mesh['parts'=2,'req'=2,'tp'=8] {'tp'}, dimensions={0} | all-to-all | bytes 40960 | tf_op jit(solution)/shard_map/all_to_all | solution.py:484
  34.2 0.0 copy-done
  34.2 0.0 slice-start.1
  34.2 0.0 copy-start.2
  34.2 1.2 %shard_map.125 = bf16[8,2,8192]{2,1,0:T(2,128)(2,1)S(1)} custom-call(s32[1]{0:T(128)} %bitcast.mine, bf16[8,2,640]{2,1,0:T(2,128)(2,1)S(1)} %all_to_all.41.x, bf16[512,8192]{1,0:T(8,128)(2,1)S(1)} %copy-done, bf16[1,16,1024]{2,1,0:T(8,128)(2,1)S(1)} %get-tuple-element.18.up_ref), custom_call_target="tpu_custom_call" | custom-call | flops 134217728 | bytes 8388608 | tf_op jit(solution)/shard_map/pallas_call | solution.py:433
  35.4 10.8 %all_to_all.42.t = bf16[8,2,8192]{2,1,0:T(2,128)(2,1)S(1)} all-to-all(bf16[8,2,8192]{2,1,0:T(2,128)(2,1)S(1)} %shard_map.125), channel_id=1, replica_groups=mesh['parts'=2,'req'=2,'tp'=8] {'tp'}, dimensions={0} | all-to-all | bytes 524288 | tf_op jit(solution)/shard_map/all_to_all | solution.py:484
  46.2 0.0 copy-done.4
  46.2 0.3 shard_map.126
  46.5 11.0 %all_to_all.43.x = bf16[8,2,8192]{2,1,0:T(2,128)(2,1)S(1)} all-to-all(bf16[8,2,8192]{2,1,0:T(2,128)(2,1)S(1)} %get-tuple-element.20), channel_id=1, replica_groups=mesh['parts'=2,'req'=2,'tp'=8] {'tp'}, dimensions={0} | all-to-all | bytes 524288 | tf_op jit(solution)/shard_map/all_to_all | solution.py:484
  57.5 0.0 slice-done
  57.5 0.0 slice-done.1
  57.5 0.0 copy-done.2
  57.5 1.5 %shard_map.127 = bf16[8,2,640]{2,1,0:T(2,128)(2,1)S(1)} custom-call(bf16[8,2,8192]{2,1,0:T(2,128)(2,1)S(1)} %all_to_all.43.x, bf16[8192,512]{1,0:T(8,128)(2,1)S(1)} %bitcast.4, bf16[8192,128]{1,0:T(8,128)(2,1)S(1)} %copy-done.2), custom_call_target="tpu_custom_call" | custom-call | flops 167772160 | bytes 10485760 | tf_op jit(solution)/shard_map/pallas_call | solution.py:159
  59.0 9.3 %all_to_all.44.refs_1_ = bf16[8,2,640]{2,1,0:T(2,128)(2,1)S(1)} all-to-all(bf16[8,2,640]{2,1,0:T(2,128)(2,1)S(1)} %shard_map.127), channel_id=1, replica_groups=mesh['parts'=2,'req'=2,'tp'=8] {'tp'}, dimensions={0} | all-to-all | bytes 40960 | tf_op jit(solution)/shard_map/all_to_all | solution.py:484
  68.3 1.9 %shard_map.128 = (bf16[8,2,640]{2,1,0:T(2,128)(2,1)S(1)}, bf16[2,2,1024]{2,1,0:T(2,128)(2,1)}) custom-call(s32[2]{0:T(128)S(1)} %copy-done.5, bf16[8,2,640]{2,1,0:T(2,128)(2,1)S(1)} %all_to_all.44.refs_1_, bf16[2,1024]{1,0:T(2,128)(2,1)S(1)} %get-tuple-element.21.refs_2_, f32[2,4,128]{2,1,0:T(4,128)S(1)} %get-tuple-element.16.refs_2_.refs_3_, ...), custom_call_target="tpu_custom_call" | custom-call | flops 33554432 | bytes 2097152 | tf_op jit(solution)/shard_map/pallas_call | solution.py:395
  70.2 9.0 %all_to_all.45.x = bf16[8,2,640]{2,1,0:T(2,128)(2,1)S(1)} all-to-all(bf16[8,2,640]{2,1,0:T(2,128)(2,1)S(1)} %get-tuple-element.23), channel_id=1, replica_groups=mesh['parts'=2,'req'=2,'tp'=8] {'tp'}, dimensions={0} | all-to-all | bytes 40960 | tf_op jit(solution)/shard_map/all_to_all | solution.py:484
  79.1 1.2 %shard_map.129 = bf16[8,2,8192]{2,1,0:T(2,128)(2,1)S(1)} custom-call(s32[1]{0:T(128)} %bitcast.mine, bf16[8,2,640]{2,1,0:T(2,128)(2,1)S(1)} %all_to_all.45.x, bf16[512,8192]{1,0:T(8,128)(2,1)S(1)} %copy-done, bf16[1,16,1024]{2,1,0:T(8,128)(2,1)S(1)} %get-tuple-element.18.up_ref), custom_call_target="tpu_custom_call" | custom-call | flops 134217728 | bytes 8388608 | tf_op jit(solution)/shard_map/pallas_call | solution.py:433
  80.4 10.7 %all_to_all.46.t = bf16[8,2,8192]{2,1,0:T(2,128)(2,1)S(1)} all-to-all(bf16[8,2,8192]{2,1,0:T(2,128)(2,1)S(1)} %shard_map.129), channel_id=1, replica_groups=mesh['parts'=2,'req'=2,'tp'=8] {'tp'}, dimensions={0} | all-to-all | bytes 524288 | tf_op jit(solution)/shard_map/all_to_all | solution.py:484
  91.0 0.1 shard_map.130
  91.1 10.8 %all_to_all.47 = bf16[8,2,8192]{2,1,0:T(2,128)(2,1)S(1)} all-to-all(bf16[8,2,8192]{2,1,0:T(2,128)(2,1)S(1)} %shard_map.130), channel_id=1, replica_groups=mesh['parts'=2,'req'=2,'tp'=8] {'tp'}, dimensions={0} | all-to-all | bytes 524288 | tf_op jit(solution)/shard_map/all_to_all | solution.py:484
  102.0 0.8 reshape.21
  (1 shorter events, 0.0 us)
Async XLA Ops:
  0.6 22.7 %collective-permute-start.1 = (bf16[64,16,1024]{2,1,0:T(8,128)(2,1)}, bf16[64,16,1024]{2,1,0:T(8,128)(2,1)S(1)}, u32[]{:S(2)}, u32[]{:S(2)}) collective-permute-start(bf16[64,16,1024]{2,1,0:T(8,128)(2,1)} %refs_7_.1), channel_id=1, source_target_pairs={{0,8},{8,0},{1,9},{9,1},{2,10},{10,2},{3,11},{11,3},{4,12},{12,4},... | collective-permute-start | bytes 6291464 | tf_op jit(solution)/shard_map/ppermute | solution.py:514
  1.1 6.6 %collective-permute-start = (bf16[64,16,512]{2,1,0:T(8,128)(2,1)}, bf16[64,16,512]{2,1,0:T(8,128)(2,1)S(1)}, u32[]{:S(2)}, u32[]{:S(2)}) collective-permute-start(bf16[64,16,512]{2,1,0:T(8,128)(2,1)} %here_ref.1), channel_id=1, source_target_pairs={{0,8},{8,0},{1,9},{9,1},{2,10},{10,2},{3,11},{11,3},{4,12},{12,4},... | collective-permute-start | bytes 3145736 | tf_op jit(solution)/shard_map/ppermute | solution.py:513
  1.9 5.8 %copy-start.3 = (bf16[64,16,512]{2,1,0:T(8,128)(2,1)S(1)}, bf16[64,16,512]{2,1,0:T(8,128)(2,1)}, u32[]{:S(2)}) copy-start(bf16[64,16,512]{2,1,0:T(8,128)(2,1)} %here_ref.1) | copy-start | bytes 3145732
  1.9 5.8 %copy-start.5 = (s32[2]{0:T(128)S(1)}, s32[2]{0:T(128)}, u32[]{:S(2)}) copy-start(s32[2]{0:T(128)} %refs_0_.3) | copy-start | bytes 28
  1.9 5.8 %copy-start.6 = (s32[128]{0:T(128)S(1)}, s32[128]{0:T(128)}, u32[]{:S(2)}) copy-start(s32[128]{0:T(128)} %refs_5_.1) | copy-start | bytes 1540
  1.9 21.4 %copy-start.1 = (bf16[2,512,1024]{2,1,0:T(8,128)(2,1)S(1)}, bf16[2,512,1024]{2,1,0:T(8,128)(2,1)}, u32[]{:S(2)}) copy-start(bf16[2,512,1024]{2,1,0:T(8,128)(2,1)} %refs_4_.2) | copy-start | bytes 6291460
  7.8 26.4 %copy-start = (bf16[512,8192]{1,0:T(8,128)(2,1)S(1)}, bf16[512,8192]{1,0:T(8,128)(2,1)}, u32[]{:S(2)}) copy-start(bf16[512,8192]{1,0:T(8,128)(2,1)} %wo.3) | copy-start | bytes 25165828
  23.3 22.9 %copy-start.4 = (bf16[8192]{0:T(1024)(128)(2,1)S(1)}, bf16[8192]{0:T(1024)(128)(2,1)}, u32[]{:S(2)}) copy-start(bf16[8192]{0:T(1024)(128)(2,1)} %param.12) | copy-start | bytes 49156
  23.3 34.2 %slice-start = ((s8[8388608]{0:T(1024)(128)(4,1)}), s8[4194304]{0:T(1024)(128)(4,1)S(1)}, s32[]{:S(2)}) async-start(s8[8388608]{0:T(1024)(128)(4,1)} %bitcast.3), calls=%async_computation.8 | async-start | bytes 8388608
  34.2 23.3 %slice-start.1 = ((s8[8388608]{0:T(1024)(128)(4,1)}), s8[4194304]{0:T(1024)(128)(4,1)S(1)}, s32[]{:S(2)}) async-start(s8[8388608]{0:T(1024)(128)(4,1)} %bitcast.3), calls=%async_computation.9 | async-start | bytes 8388608
  34.2 23.3 %copy-start.2 = (bf16[8192,128]{1,0:T(8,128)(2,1)S(1)}, bf16[8192,128]{1,0:T(8,128)(2,1)}, u32[]{:S(2)}) copy-start(bf16[8192,128]{1,0:T(8,128)(2,1)} %wp.3) | copy-start | bytes 6291460
where the time goes:
time: 103 us
  blocking collectives  85.6 us (83%)
  Pallas kernels  14.3 us (14%)
  between operations  1.42 us (1%)
    all_to_all x8, blocking collectives, exchange(): return lax.all_to_all(chunks, 'tp', split_axis=0, concat_axis=0, tiled=True)  85.6 us
    pallas_call x1, Pallas kernels, first_projection(): pl.pallas_call(body, out_shape=(jax.ShapeDtypeStruct((shares, own, messag...  5.79 us
    pallas_call x2, Pallas kernels, attend(): pl.pallas_call(body, out_shape=tuple(outs), in_specs=specs, out_specs=(wh...  3.49 us
    pallas_call x2, Pallas kernels, output_terms(): pl.pallas_call(body, out_shape=jax.ShapeDtypeStruct((shares, own, width),...  2.48 us
  transfers between devices with their start and end apart: 2, of which 0 were waited for; matrix products, arithmetic and copies ran while one was open for 0% of the time, Pallas kernels for 6%

commit v1 on v0

--- a/solution.py
+++ b/solution.py
@@ -245,7 +245,7 @@
     groups = QUERY_HEAD_COUNT // KV_HEADS
     lines = groups * own
     pair_inside = pairs is None
-    first, last = step == 0, step == STEPS - 1
+    first = step == 0
     shrink = 1.0 / math.sqrt(HEAD_SIZE)
 
     def body(*refs):
@@ -292,11 +292,7 @@
         keys = [turn(pair_head(g), cosine, sine).astype(bf16) for g in range(KV_HEADS)]
         values = [pair_head(KV_HEADS + g).astype(bf16) for g in range(KV_HEADS)]
         fresh = jnp.concatenate(keys + values, axis=1)
-        if last:
-            new[0] = old[...]
-            new[1] = fresh
-        else:
-            new[...] = fresh
+        new[...] = fresh
         wide_cosine, wide_sine = spread(cosine), spread(sine)
         valid = lax.broadcasted_iota(jnp.int32, (lines, context), 1) < by_row(
             [jnp.full((lines, 1), lens[r], jnp.int32) for r in range(own)]
@@ -379,7 +375,7 @@
         specs.append(whole())
     outs = [
         jax.ShapeDtypeStruct((shares, own, query_width + HEAD_SIZE), bf16),
-        jax.ShapeDtypeStruct((STEPS, own, width) if last else (own, width), bf16),
+        jax.ShapeDtypeStruct((own, width), bf16),
     ]
     scratch = []
     if first:
@@ -405,14 +401,24 @@
     )(*operands)
 
 
-def output_terms(arrived, output_weight, up):
+def output_terms(arrived, output_weight, up, pairs):
     shares, own, _ = arrived.shape
     query_width, width = output_weight.shape
     blocks, rank, share_width = up.shape
     rows = shares * own
     step = 1024
 
-    def body(mine, x, wo, up_ref, out, added):
+    count = len(pairs)
+
+    def body(mine, x, wo, up_ref, *refs):
+        given, refs = refs[:count], refs[count:]
+        out, added = refs[0], refs[1 + bool(count)]
+        copies = [
+            pltpu.make_async_copy(pair, refs[1].at[n], refs[3].at[n])
+            for n, pair in enumerate(given)
+        ]
+        for copy in copies:
+            copy.start()
         heads = rows_of(x, 0, query_width)
         low = rows_of(x, query_width, HEAD_SIZE)[:, :rank]
         added[...] = jnp.zeros_like(added)
@@ -429,16 +435,25 @@
             )
             for j in range(shares):
                 out[j, :, columns] = total[j * own : (j + 1) * own, :].astype(out.dtype)
-
+        for copy in copies:
+            copy.wait()
+
+    outs = [jax.ShapeDtypeStruct((shares, own, width), term_type)]
+    out_specs = [whole()]
+    scratch = [pltpu.VMEM((rows, width), f32)]
+    if count:
+        outs.append(jax.ShapeDtypeStruct((count,) + pairs[0].shape, bf16))
+        out_specs.append(whole(pltpu.HBM))
+        scratch.append(pltpu.SemaphoreType.DMA((count,)))
     return pl.pallas_call(
         body,
-        out_shape=jax.ShapeDtypeStruct((shares, own, width), term_type),
-        in_specs=[whole(pltpu.SMEM)] + [whole()] * 3,
-        out_specs=whole(),
-        scratch_shapes=[pltpu.VMEM((rows, width), f32)],
+        out_shape=tuple(outs),
+        in_specs=[whole(pltpu.SMEM)] + [whole()] * 3 + [whole(pl.ANY)] * count,
+        out_specs=tuple(out_specs),
+        scratch_shapes=scratch,
         compiler_params=pltpu.CompilerParams(vmem_limit_bytes=16 * MIB),
         cost_estimate=cost(2 * rows * width * query_width, 2 * width * query_width),
-    )(own_index("tp"), arrived, output_weight, up)
+    )(own_index("tp"), arrived, output_weight, up, *pairs)
 
 
 def close_step(terms, hidden, scale):
@@ -519,6 +534,7 @@
         message, adapters, adapter_down_projection, other_down, lengths, blocks
     )
     down = fresh = None
+    made = []
     for step in range(STEPS):
         arrived = exchange(message)
         start = 0 if step else lead
@@ -531,13 +547,17 @@
         )
         if not step:
             down, up = kept
-        terms = exchange(output_terms(exchange(attended), output_weight, up))
+        made.append(fresh)
+        terms, *new_pairs = output_terms(
+            exchange(attended), output_weight, up, made if step == STEPS - 1 else []
+        )
+        terms = exchange(terms)
         if step < STEPS - 1:
             spread, hidden = close_step(terms, hidden, scale)
             message = next_projection(exchange(spread), weights)
         else:
             (spread,) = close_step(terms, hidden, None)
-    return (exchange(spread).reshape(rows_req, width), fresh)
+    return (exchange(spread).reshape(rows_req, width), new_pairs[0])
 
 
 def solution(mesh):

time: 103 us -> 104 us (level); the launches traced: 103 us -> 102 us
  no operation moved by 1% of the time
where the time goes in v1:
time: 104 us; the launch traced here: 102 us
  blocking collectives  85.7 us (82%)
  Pallas kernels  13.8 us (13%)
  between operations  1.43 us (1%)
    all_to_all x8, blocking collectives, exchange(): return lax.all_to_all(chunks, 'tp', split_axis=0, concat_axis=0, tiled=True)  85.7 us
    pallas_call x1, Pallas kernels, first_projection(): pl.pallas_call(body, out_shape=(jax.ShapeDtypeStruct((shares, own, messag...  5.79 us
    pallas_call x2, Pallas kernels, attend(): pl.pallas_call(body, out_shape=tuple(outs), in_specs=specs, out_specs=(wh...  3.02 us
    pallas_call x2, Pallas kernels, output_terms(): pl.pallas_call(body, out_shape=tuple(outs), in_specs=[whole(pltpu.SMEM)]...  2.51 us
  transfers between devices with their start and end apart: 2, of which 0 were waited for; matrix products, arithmetic and copies ran while one was open for 0% of the time, Pallas kernels for 6%

profile of v1, /device:TPU:0, one launch (start us, length us, event | category | flops | bytes accessed | tf_op | source)
XLA Modules:
  0.0 102.3 jit_solution(13308842056907831550)
XLA Ops:
  0.6 0.5 collective-permute-start.1
  1.1 0.1 collective-permute-start
  1.9 0.0 copy-start.3
  1.9 0.0 copy-start.5
  1.9 0.0 copy-start.6
  1.9 0.0 copy-start.1
  1.9 5.8 %shard_map.122 = (bf16[8,2,640]{2,1,0:T(2,128)(2,1)S(1)}, bf16[2,8192]{1,0:T(2,128)(2,1)S(1)}) custom-call(s32[1]{0:T(128)} %bitcast.mine, bf16[16,8192]{1,0:T(8,128)(2,1)} %source_ref.1, bf16[64,128]{1,0:T(8,128)(2,1)} %bitcast.5, bf16[8192,512]{1,0:T(8,128)(2,1)} %wq.3, bf16[8192,128]{1,0:T(8,128)(2,1)} %wp.3), custom_call_target="tpu_custom_call" | custom-call | flops 167772160 | bytes 10485760 | tf_op jit(solution)/shard_map/pallas_call | solution.py:129
  7.7 0.0 collective-permute-done.other_ref
  7.7 0.0 copy-done.3
  7.7 0.0 copy-done.5
  7.7 0.0 copy-done.6
  7.8 0.0 copy-start
  7.8 0.7 shard_map.123
  8.5 14.8 %all_to_all.40.refs_1_ = bf16[8,2,4736]{2,1,0:T(2,128)(2,1)S(1)} all-to-all(bf16[8,2,4736]{2,1,0:T(2,128)(2,1)S(1)} %get-tuple-element.17), channel_id=1, replica_groups=mesh['parts'=2,'req'=2,'tp'=8] {'tp'}, dimensions={0} | all-to-all | bytes 303104 | tf_op jit(solution)/shard_map/all_to_all | solution.py:499
  23.3 0.0 collective-permute-done.1.refs_8_
  23.3 0.0 copy-done.1
  23.3 0.0 copy-start.4
  23.3 0.0 slice-start
  23.3 1.6 %shard_map.124 = (bf16[8,2,640]{2,1,0:T(2,128)(2,1)S(1)}, bf16[2,1024]{1,0:T(2,128)(2,1)S(1)}, bf16[8,16,512]{2,1,0:T(8,128)(2,1)S(1)}, bf16[1,16,1024]{2,1,0:T(8,128)(2,1)S(1)}) custom-call(s32[2]{0:T(128)S(1)} %copy-done.5, bf16[8,2,4736]{2,1,0:T(2,128)(2,1)S(1)} %all_to_all.40.refs_1_, f32[2,4,128]{2,1,0:T(4,128)S(1)} %get-tuple-element.18.refs_2_.refs_3_, ...), custom_call_target="tpu_custom_call" | custom-call | flops 33554432 | bytes 2097152 | tf_op jit(solution)/shard_map/pallas_call | solution.py:391
  24.9 9.3 %all_to_all.41.x = bf16[8,2,640]{2,1,0:T(2,128)(2,1)S(1)} all-to-all(bf16[8,2,640]{2,1,0:T(2,128)(2,1)S(1)} %get-tuple-element.19), channel_id=1, replica_groups=mesh['parts'=2,'req'=2,'tp'=8] {'tp'}, dimensions={0} | all-to-all | bytes 40960 | tf_op jit(solution)/shard_map/all_to_all | solution.py:499
  34.1 0.0 copy-done
  34.1 0.0 slice-start.1
  34.1 0.0 copy-start.2
  34.1 1.2 %shard_map.125 = bf16[8,2,8192]{2,1,0:T(2,128)(2,1)S(1)} custom-call(s32[1]{0:T(128)} %bitcast.mine, bf16[8,2,640]{2,1,0:T(2,128)(2,1)S(1)} %all_to_all.41.x, bf16[512,8192]{1,0:T(8,128)(2,1)S(1)} %copy-done, bf16[1,16,1024]{2,1,0:T(8,128)(2,1)S(1)} %get-tuple-element.20.up_ref), custom_call_target="tpu_custom_call" | custom-call | flops 134217728 | bytes 8388608 | tf_op jit(solution)/shard_map/pallas_call | solution.py:448
  35.4 10.8 %all_to_all.42.t = bf16[8,2,8192]{2,1,0:T(2,128)(2,1)S(1)} all-to-all(bf16[8,2,8192]{2,1,0:T(2,128)(2,1)S(1)} %shard_map.125), channel_id=1, replica_groups=mesh['parts'=2,'req'=2,'tp'=8] {'tp'}, dimensions={0} | all-to-all | bytes 524288 | tf_op jit(solution)/shard_map/all_to_all | solution.py:499
  46.2 0.0 copy-done.4
  46.2 0.3 shard_map.126
  46.4 11.0 %all_to_all.43.x = bf16[8,2,8192]{2,1,0:T(2,128)(2,1)S(1)} all-to-all(bf16[8,2,8192]{2,1,0:T(2,128)(2,1)S(1)} %get-tuple-element.22), channel_id=1, replica_groups=mesh['parts'=2,'req'=2,'tp'=8] {'tp'}, dimensions={0} | all-to-all | bytes 524288 | tf_op jit(solution)/shard_map/all_to_all | solution.py:499
  57.4 0.0 slice-done
  57.4 0.0 slice-done.1
  57.4 0.0 copy-done.2
  57.4 1.5 %shard_map.127 = bf16[8,2,640]{2,1,0:T(2,128)(2,1)S(1)} custom-call(bf16[8,2,8192]{2,1,0:T(2,128)(2,1)S(1)} %all_to_all.43.x, bf16[8192,512]{1,0:T(8,128)(2,1)S(1)} %bitcast.4, bf16[8192,128]{1,0:T(8,128)(2,1)S(1)} %copy-done.2), custom_call_target="tpu_custom_call" | custom-call | flops 167772160 | bytes 10485760 | tf_op jit(solution)/shard_map/pallas_call | solution.py:159
  58.9 9.3 %all_to_all.44.refs_1_ = bf16[8,2,640]{2,1,0:T(2,128)(2,1)S(1)} all-to-all(bf16[8,2,640]{2,1,0:T(2,128)(2,1)S(1)} %shard_map.127), channel_id=1, replica_groups=mesh['parts'=2,'req'=2,'tp'=8] {'tp'}, dimensions={0} | all-to-all | bytes 40960 | tf_op jit(solution)/shard_map/all_to_all | solution.py:499
  68.2 1.5 %shard_map.128 = (bf16[8,2,640]{2,1,0:T(2,128)(2,1)S(1)}, bf16[2,1024]{1,0:T(2,128)(2,1)S(1)}) custom-call(s32[2]{0:T(128)S(1)} %copy-done.5, bf16[8,2,640]{2,1,0:T(2,128)(2,1)S(1)} %all_to_all.44.refs_1_, bf16[2,1024]{1,0:T(2,128)(2,1)S(1)} %get-tuple-element.23.refs_2_.refs_0_, f32[2,4,128]{2,1,0:T(4,128)S(1)} %get-tuple-element.18.refs_2_.refs_3_, ...), custom_call_target="tpu_custom_call" | custom-call | flops 33554432 | bytes 2097152 | tf_op jit(solution)/shard_map/pallas_call | solution.py:391
  69.7 9.0 %all_to_all.45.x = bf16[8,2,640]{2,1,0:T(2,128)(2,1)S(1)} all-to-all(bf16[8,2,640]{2,1,0:T(2,128)(2,1)S(1)} %get-tuple-element.25), channel_id=1, replica_groups=mesh['parts'=2,'req'=2,'tp'=8] {'tp'}, dimensions={0} | all-to-all | bytes 40960 | tf_op jit(solution)/shard_map/all_to_all | solution.py:499
  78.7 1.3 %shard_map.129 = (bf16[8,2,8192]{2,1,0:T(2,128)(2,1)S(1)}, bf16[2,2,1024]{2,1,0:T(2,128)(2,1)}) custom-call(s32[1]{0:T(128)} %bitcast.mine, bf16[8,2,640]{2,1,0:T(2,128)(2,1)S(1)} %all_to_all.45.x, bf16[512,8192]{1,0:T(8,128)(2,1)S(1)} %copy-done, bf16[1,16,1024]{2,1,0:T(8,128)(2,1)S(1)} %get-tuple-element.20.up_ref, ...), custom_call_target="tpu_custom_call" | custom-call | flops 134217728 | bytes 8388608 | tf_op jit(solution)/shard_map/pallas_call | solution.py:448
  79.9 10.7 %all_to_all.46.t = bf16[8,2,8192]{2,1,0:T(2,128)(2,1)S(1)} all-to-all(bf16[8,2,8192]{2,1,0:T(2,128)(2,1)S(1)} %get-tuple-element.27), channel_id=1, replica_groups=mesh['parts'=2,'req'=2,'tp'=8] {'tp'}, dimensions={0} | all-to-all | bytes 524288 | tf_op jit(solution)/shard_map/all_to_all | solution.py:499
  90.6 0.1 shard_map.130
  90.7 10.8 %all_to_all.47 = bf16[8,2,8192]{2,1,0:T(2,128)(2,1)S(1)} all-to-all(bf16[8,2,8192]{2,1,0:T(2,128)(2,1)S(1)} %shard_map.130), channel_id=1, replica_groups=mesh['parts'=2,'req'=2,'tp'=8] {'tp'}, dimensions={0} | all-to-all | bytes 524288 | tf_op jit(solution)/shard_map/all_to_all | solution.py:499
  101.5 0.8 reshape.21
  (1 shorter events, 0.0 us)
Async XLA Ops:
  0.6 22.7 %collective-permute-start.1 = (bf16[64,16,1024]{2,1,0:T(8,128)(2,1)}, bf16[64,16,1024]{2,1,0:T(8,128)(2,1)S(1)}, u32[]{:S(2)}, u32[]{:S(2)}) collective-permute-start(bf16[64,16,1024]{2,1,0:T(8,128)(2,1)} %refs_7_.1), channel_id=1, source_target_pairs={{0,8},{8,0},{1,9},{9,1},{2,10},{10,2},{3,11},{11,3},{4,12},{12,4},... | collective-permute-start | bytes 6291464 | tf_op jit(solution)/shard_map/ppermute | solution.py:529
  1.1 6.6 %collective-permute-start = (bf16[64,16,512]{2,1,0:T(8,128)(2,1)}, bf16[64,16,512]{2,1,0:T(8,128)(2,1)S(1)}, u32[]{:S(2)}, u32[]{:S(2)}) collective-permute-start(bf16[64,16,512]{2,1,0:T(8,128)(2,1)} %here_ref.1), channel_id=1, source_target_pairs={{0,8},{8,0},{1,9},{9,1},{2,10},{10,2},{3,11},{11,3},{4,12},{12,4},... | collective-permute-start | bytes 3145736 | tf_op jit(solution)/shard_map/ppermute | solution.py:528
  1.9 5.8 %copy-start.3 = (bf16[64,16,512]{2,1,0:T(8,128)(2,1)S(1)}, bf16[64,16,512]{2,1,0:T(8,128)(2,1)}, u32[]{:S(2)}) copy-start(bf16[64,16,512]{2,1,0:T(8,128)(2,1)} %here_ref.1) | copy-start | bytes 3145732
  1.9 5.8 %copy-start.5 = (s32[2]{0:T(128)S(1)}, s32[2]{0:T(128)}, u32[]{:S(2)}) copy-start(s32[2]{0:T(128)} %refs_0_.3) | copy-start | bytes 28
  1.9 5.8 %copy-start.6 = (s32[128]{0:T(128)S(1)}, s32[128]{0:T(128)}, u32[]{:S(2)}) copy-start(s32[128]{0:T(128)} %refs_5_.1) | copy-start | bytes 1540
  1.9 21.4 %copy-start.1 = (bf16[2,512,1024]{2,1,0:T(8,128)(2,1)S(1)}, bf16[2,512,1024]{2,1,0:T(8,128)(2,1)}, u32[]{:S(2)}) copy-start(bf16[2,512,1024]{2,1,0:T(8,128)(2,1)} %refs_4_.2) | copy-start | bytes 6291460
  7.8 26.4 %copy-start = (bf16[512,8192]{1,0:T(8,128)(2,1)S(1)}, bf16[512,8192]{1,0:T(8,128)(2,1)}, u32[]{:S(2)}) copy-start(bf16[512,8192]{1,0:T(8,128)(2,1)} %wo.3) | copy-start | bytes 25165828
  23.3 22.9 %copy-start.4 = (bf16[8192]{0:T(1024)(128)(2,1)S(1)}, bf16[8192]{0:T(1024)(128)(2,1)}, u32[]{:S(2)}) copy-start(bf16[8192]{0:T(1024)(128)(2,1)} %param.12) | copy-start | bytes 49156
  23.3 34.1 %slice-start = ((s8[8388608]{0:T(1024)(128)(4,1)}), s8[4194304]{0:T(1024)(128)(4,1)S(1)}, s32[]{:S(2)}) async-start(s8[8388608]{0:T(1024)(128)(4,1)} %bitcast.3), calls=%async_computation.8 | async-start | bytes 8388608
  34.1 23.3 %slice-start.1 = ((s8[8388608]{0:T(1024)(128)(4,1)}), s8[4194304]{0:T(1024)(128)(4,1)S(1)}, s32[]{:S(2)}) async-start(s8[8388608]{0:T(1024)(128)(4,1)} %bitcast.3), calls=%async_computation.9 | async-start | bytes 8388608
  34.1 23.3 %copy-start.2 = (bf16[8192,128]{1,0:T(8,128)(2,1)S(1)}, bf16[8192,128]{1,0:T(8,128)(2,1)}, u32[]{:S(2)}) copy-start(bf16[8192,128]{1,0:T(8,128)(2,1)} %wp.3) | copy-start | bytes 6291460

commit v2 on v1

--- a/solution.py
+++ b/solution.py
@@ -81,7 +81,7 @@
     shares = rows // own
     message = sum(w.shape[1] for w in weights)
     pieces = pieces_of(width, 4)
-    ahead = 2
+    ahead = 3
 
     def body(mine, source_ref, s, wq, wp, out, held, *scratch):
         kept_q, kept_p, sems, x, gains, wide, normed, pre = scratch

time: 104 us -> 103 us (level)
  no operation moved by 1% of the time
where the time goes in v2:
time: 103 us; the launch traced here: 102 us
  blocking collectives  85.7 us (83%)
  Pallas kernels  13.7 us (13%)
  between operations  1.43 us (1%)
    all_to_all x8, blocking collectives, exchange(): return lax.all_to_all(chunks, 'tp', split_axis=0, concat_axis=0, tiled=True)  85.7 us
    pallas_call x1, Pallas kernels, first_projection(): pl.pallas_call(body, out_shape=(jax.ShapeDtypeStruct((shares, own, messag...  5.72 us
    pallas_call x2, Pallas kernels, attend(): pl.pallas_call(body, out_shape=tuple(outs), in_specs=specs, out_specs=(wh...  3.02 us
    pallas_call x2, Pallas kernels, output_terms(): pl.pallas_call(body, out_shape=tuple(outs), in_specs=[whole(pltpu.SMEM)]...  2.51 us
  transfers between devices with their start and end apart: 2, of which 0 were waited for; matrix products, arithmetic and copies ran while one was open for 0% of the time, Pallas kernels for 6%

profile of v2, /device:TPU:0, one launch (start us, length us, event | category | flops | bytes accessed | tf_op | source)
XLA Modules:
  0.0 102.3 jit_solution(3247178514130841371)
XLA Ops:
  0.6 0.5 collective-permute-start.1
  1.1 0.1 collective-permute-start
  1.9 0.0 copy-start.3
  1.9 0.0 copy-start.5
  1.9 0.0 copy-start.6
  1.9 0.0 copy-start.1
  1.9 5.7 %shard_map.122 = (bf16[8,2,640]{2,1,0:T(2,128)(2,1)S(1)}, bf16[2,8192]{1,0:T(2,128)(2,1)S(1)}) custom-call(s32[1]{0:T(128)} %bitcast.mine, bf16[16,8192]{1,0:T(8,128)(2,1)} %source_ref.1, bf16[64,128]{1,0:T(8,128)(2,1)} %bitcast.5, bf16[8192,512]{1,0:T(8,128)(2,1)} %wq.3, bf16[8192,128]{1,0:T(8,128)(2,1)} %wp.3), custom_call_target="tpu_custom_call" | custom-call | flops 167772160 | bytes 10485760 | tf_op jit(solution)/shard_map/pallas_call | solution.py:129
  7.7 0.0 collective-permute-done.other_ref
  7.7 0.0 copy-done.3
  7.7 0.0 copy-done.5
  7.7 0.0 copy-done.6
  7.7 0.0 copy-start
  7.7 0.7 shard_map.123
  8.4 14.8 %all_to_all.40.refs_1_ = bf16[8,2,4736]{2,1,0:T(2,128)(2,1)S(1)} all-to-all(bf16[8,2,4736]{2,1,0:T(2,128)(2,1)S(1)} %get-tuple-element.17), channel_id=1, replica_groups=mesh['parts'=2,'req'=2,'tp'=8] {'tp'}, dimensions={0} | all-to-all | bytes 303104 | tf_op jit(solution)/shard_map/all_to_all | solution.py:499
  23.2 0.0 collective-permute-done.1.refs_8_
  23.2 0.0 copy-done.1
  23.2 0.0 copy-start.4
  23.2 0.0 slice-start
  23.3 1.6 %shard_map.124 = (bf16[8,2,640]{2,1,0:T(2,128)(2,1)S(1)}, bf16[2,1024]{1,0:T(2,128)(2,1)S(1)}, bf16[8,16,512]{2,1,0:T(8,128)(2,1)S(1)}, bf16[1,16,1024]{2,1,0:T(8,128)(2,1)S(1)}) custom-call(s32[2]{0:T(128)S(1)} %copy-done.5, bf16[8,2,4736]{2,1,0:T(2,128)(2,1)S(1)} %all_to_all.40.refs_1_, f32[2,4,128]{2,1,0:T(4,128)S(1)} %get-tuple-element.18.refs_2_.refs_3_, ...), custom_call_target="tpu_custom_call" | custom-call | flops 33554432 | bytes 2097152 | tf_op jit(solution)/shard_map/pallas_call | solution.py:391
  24.8 9.3 %all_to_all.41.x = bf16[8,2,640]{2,1,0:T(2,128)(2,1)S(1)} all-to-all(bf16[8,2,640]{2,1,0:T(2,128)(2,1)S(1)} %get-tuple-element.19), channel_id=1, replica_groups=mesh['parts'=2,'req'=2,'tp'=8] {'tp'}, dimensions={0} | all-to-all | bytes 40960 | tf_op jit(solution)/shard_map/all_to_all | solution.py:499
  34.1 0.0 copy-done
  34.1 0.0 slice-start.1
  34.1 0.0 copy-start.2
  34.1 1.2 %shard_map.125 = bf16[8,2,8192]{2,1,0:T(2,128)(2,1)S(1)} custom-call(s32[1]{0:T(128)} %bitcast.mine, bf16[8,2,640]{2,1,0:T(2,128)(2,1)S(1)} %all_to_all.41.x, bf16[512,8192]{1,0:T(8,128)(2,1)S(1)} %copy-done, bf16[1,16,1024]{2,1,0:T(8,128)(2,1)S(1)} %get-tuple-element.20.up_ref), custom_call_target="tpu_custom_call" | custom-call | flops 134217728 | bytes 8388608 | tf_op jit(solution)/shard_map/pallas_call | solution.py:448
  35.3 10.8 %all_to_all.42.t = bf16[8,2,8192]{2,1,0:T(2,128)(2,1)S(1)} all-to-all(bf16[8,2,8192]{2,1,0:T(2,128)(2,1)S(1)} %shard_map.125), channel_id=1, replica_groups=mesh['parts'=2,'req'=2,'tp'=8] {'tp'}, dimensions={0} | all-to-all | bytes 524288 | tf_op jit(solution)/shard_map/all_to_all | solution.py:499
  46.1 0.0 copy-done.4
  46.1 0.3 shard_map.126
  46.4 11.0 %all_to_all.43.x = bf16[8,2,8192]{2,1,0:T(2,128)(2,1)S(1)} all-to-all(bf16[8,2,8192]{2,1,0:T(2,128)(2,1)S(1)} %get-tuple-element.22), channel_id=1, replica_groups=mesh['parts'=2,'req'=2,'tp'=8] {'tp'}, dimensions={0} | all-to-all | bytes 524288 | tf_op jit(solution)/shard_map/all_to_all | solution.py:499
  57.3 0.0 slice-done
  57.4 0.0 slice-done.1
  57.4 0.0 copy-done.2
  57.4 1.5 %shard_map.127 = bf16[8,2,640]{2,1,0:T(2,128)(2,1)S(1)} custom-call(bf16[8,2,8192]{2,1,0:T(2,128)(2,1)S(1)} %all_to_all.43.x, bf16[8192,512]{1,0:T(8,128)(2,1)S(1)} %bitcast.4, bf16[8192,128]{1,0:T(8,128)(2,1)S(1)} %copy-done.2), custom_call_target="tpu_custom_call" | custom-call | flops 167772160 | bytes 10485760 | tf_op jit(solution)/shard_map/pallas_call | solution.py:159
  58.9 9.3 %all_to_all.44.refs_1_ = bf16[8,2,640]{2,1,0:T(2,128)(2,1)S(1)} all-to-all(bf16[8,2,640]{2,1,0:T(2,128)(2,1)S(1)} %shard_map.127), channel_id=1, replica_groups=mesh['parts'=2,'req'=2,'tp'=8] {'tp'}, dimensions={0} | all-to-all | bytes 40960 | tf_op jit(solution)/shard_map/all_to_all | solution.py:499
  68.1 1.5 %shard_map.128 = (bf16[8,2,640]{2,1,0:T(2,128)(2,1)S(1)}, bf16[2,1024]{1,0:T(2,128)(2,1)S(1)}) custom-call(s32[2]{0:T(128)S(1)} %copy-done.5, bf16[8,2,640]{2,1,0:T(2,128)(2,1)S(1)} %all_to_all.44.refs_1_, bf16[2,1024]{1,0:T(2,128)(2,1)S(1)} %get-tuple-element.23.refs_2_.refs_0_, f32[2,4,128]{2,1,0:T(4,128)S(1)} %get-tuple-element.18.refs_2_.refs_3_, ...), custom_call_target="tpu_custom_call" | custom-call | flops 33554432 | bytes 2097152 | tf_op jit(solution)/shard_map/pallas_call | solution.py:391
  69.6 9.0 %all_to_all.45.x = bf16[8,2,640]{2,1,0:T(2,128)(2,1)S(1)} all-to-all(bf16[8,2,640]{2,1,0:T(2,128)(2,1)S(1)} %get-tuple-element.25), channel_id=1, replica_groups=mesh['parts'=2,'req'=2,'tp'=8] {'tp'}, dimensions={0} | all-to-all | bytes 40960 | tf_op jit(solution)/shard_map/all_to_all | solution.py:499
  78.6 1.3 %shard_map.129 = (bf16[8,2,8192]{2,1,0:T(2,128)(2,1)S(1)}, bf16[2,2,1024]{2,1,0:T(2,128)(2,1)}) custom-call(s32[1]{0:T(128)} %bitcast.mine, bf16[8,2,640]{2,1,0:T(2,128)(2,1)S(1)} %all_to_all.45.x, bf16[512,8192]{1,0:T(8,128)(2,1)S(1)} %copy-done, bf16[1,16,1024]{2,1,0:T(8,128)(2,1)S(1)} %get-tuple-element.20.up_ref, ...), custom_call_target="tpu_custom_call" | custom-call | flops 134217728 | bytes 8388608 | tf_op jit(solution)/shard_map/pallas_call | solution.py:448
  79.9 10.7 %all_to_all.46.t = bf16[8,2,8192]{2,1,0:T(2,128)(2,1)S(1)} all-to-all(bf16[8,2,8192]{2,1,0:T(2,128)(2,1)S(1)} %get-tuple-element.27), channel_id=1, replica_groups=mesh['parts'=2,'req'=2,'tp'=8] {'tp'}, dimensions={0} | all-to-all | bytes 524288 | tf_op jit(solution)/shard_map/all_to_all | solution.py:499
  90.5 0.1 shard_map.130
  90.6 10.8 %all_to_all.47 = bf16[8,2,8192]{2,1,0:T(2,128)(2,1)S(1)} all-to-all(bf16[8,2,8192]{2,1,0:T(2,128)(2,1)S(1)} %shard_map.130), channel_id=1, replica_groups=mesh['parts'=2,'req'=2,'tp'=8] {'tp'}, dimensions={0} | all-to-all | bytes 524288 | tf_op jit(solution)/shard_map/all_to_all | solution.py:499
  101.5 0.8 reshape.21
  (1 shorter events, 0.0 us)
Async XLA Ops:
  0.6 22.6 %collective-permute-start.1 = (bf16[64,16,1024]{2,1,0:T(8,128)(2,1)}, bf16[64,16,1024]{2,1,0:T(8,128)(2,1)S(1)}, u32[]{:S(2)}, u32[]{:S(2)}) collective-permute-start(bf16[64,16,1024]{2,1,0:T(8,128)(2,1)} %refs_7_.1), channel_id=1, source_target_pairs={{0,8},{8,0},{1,9},{9,1},{2,10},{10,2},{3,11},{11,3},{4,12},{12,4},... | collective-permute-start | bytes 6291464 | tf_op jit(solution)/shard_map/ppermute | solution.py:529
  1.1 6.5 %collective-permute-start = (bf16[64,16,512]{2,1,0:T(8,128)(2,1)}, bf16[64,16,512]{2,1,0:T(8,128)(2,1)S(1)}, u32[]{:S(2)}, u32[]{:S(2)}) collective-permute-start(bf16[64,16,512]{2,1,0:T(8,128)(2,1)} %here_ref.1), channel_id=1, source_target_pairs={{0,8},{8,0},{1,9},{9,1},{2,10},{10,2},{3,11},{11,3},{4,12},{12,4},... | collective-permute-start | bytes 3145736 | tf_op jit(solution)/shard_map/ppermute | solution.py:528
  1.9 5.8 %copy-start.3 = (bf16[64,16,512]{2,1,0:T(8,128)(2,1)S(1)}, bf16[64,16,512]{2,1,0:T(8,128)(2,1)}, u32[]{:S(2)}) copy-start(bf16[64,16,512]{2,1,0:T(8,128)(2,1)} %here_ref.1) | copy-start | bytes 3145732
  1.9 5.8 %copy-start.5 = (s32[2]{0:T(128)S(1)}, s32[2]{0:T(128)}, u32[]{:S(2)}) copy-start(s32[2]{0:T(128)} %refs_0_.3) | copy-start | bytes 28
  1.9 5.8 %copy-start.6 = (s32[128]{0:T(128)S(1)}, s32[128]{0:T(128)}, u32[]{:S(2)}) copy-start(s32[128]{0:T(128)} %refs_5_.1) | copy-start | bytes 1540
  1.9 21.3 %copy-start.1 = (bf16[2,512,1024]{2,1,0:T(8,128)(2,1)S(1)}, bf16[2,512,1024]{2,1,0:T(8,128)(2,1)}, u32[]{:S(2)}) copy-start(bf16[2,512,1024]{2,1,0:T(8,128)(2,1)} %refs_4_.2) | copy-start | bytes 6291460
  7.7 26.4 %copy-start = (bf16[512,8192]{1,0:T(8,128)(2,1)S(1)}, bf16[512,8192]{1,0:T(8,128)(2,1)}, u32[]{:S(2)}) copy-start(bf16[512,8192]{1,0:T(8,128)(2,1)} %wo.3) | copy-start | bytes 25165828
  23.2 22.9 %copy-start.4 = (bf16[8192]{0:T(1024)(128)(2,1)S(1)}, bf16[8192]{0:T(1024)(128)(2,1)}, u32[]{:S(2)}) copy-start(bf16[8192]{0:T(1024)(128)(2,1)} %param.12) | copy-start | bytes 49156
  23.2 34.1 %slice-start = ((s8[8388608]{0:T(1024)(128)(4,1)}), s8[4194304]{0:T(1024)(128)(4,1)S(1)}, s32[]{:S(2)}) async-start(s8[8388608]{0:T(1024)(128)(4,1)} %bitcast.3), calls=%async_computation.8 | async-start | bytes 8388608
  34.1 23.3 %slice-start.1 = ((s8[8388608]{0:T(1024)(128)(4,1)}), s8[4194304]{0:T(1024)(128)(4,1)S(1)}, s32[]{:S(2)}) async-start(s8[8388608]{0:T(1024)(128)(4,1)} %bitcast.3), calls=%async_computation.9 | async-start | bytes 8388608
  34.1 23.3 %copy-start.2 = (bf16[8192,128]{1,0:T(8,128)(2,1)S(1)}, bf16[8192,128]{1,0:T(8,128)(2,1)}, u32[]{:S(2)}) copy-start(bf16[8192,128]{1,0:T(8,128)(2,1)} %wp.3) | copy-start | bytes 6291460
